TPU v7x, 128 devices: a whole 4x4x4 slice. The times are simulated.
128 devices in a mesh: blk: 32 (over y, z, core), face: 4 (over x).
Axes of the slice: x: 4, y: 4, z: 4, core: 2. Of those that a mesh axis runs over, the one named last changes fastest.
Arguments:
- forcing: float32 [32, 4, 3, 64, 4096], P('blk', 'face'), may hold values from -6 to 6
- modulus: float32 [32, 4, 3], P('blk', 'face'), may hold values from 0.5 to 4
- orient_codes: int32 [32, 4], P('blk', 'face'), may hold values from 0 to 3
Outputs:
- displacement: float32 [32, 4, 3, 64, 4096], P('blk', 'face')
All inputs are finite; a program needn't handle non-finite values.
Results may differ from a plain program's by a relative error of at most 0.0001.
Values sent between devices are 32-bit elements; how exact they have to be, the bound alone decides.
A program may use at most 128 MiB of HBM per device.

v0:
```python
import functools
import math

import jax
import jax.numpy as jnp
import ml_dtypes
import numpy as np
from jax import lax
from jax.experimental import pallas as pl
from jax.experimental.pallas import tpu as pltpu
from jax.sharding import PartitionSpec as P

N = 64
ITERS = 2
COMPS = 3
MESH = pl.DeviceIdType.MESH
F32 = jnp.float32
BF16 = jnp.bfloat16
mass_shift = 0.02
inject_scale = 2.0
traction_mix = 0.5
penalty_mix = 0.25
lower_edge = 0.3
upper_edge = 1.5


def split_np(a):
    a = np.asarray(a, np.float32)
    hi = a.astype(ml_dtypes.bfloat16)
    lo = (a - hi.astype(np.float32)).astype(ml_dtypes.bfloat16)
    return hi, lo


def rows3(a):
    hi, lo = split_np(a)
    return np.concatenate([hi, hi, lo], axis=1)


def square3(a):
    hi, lo = split_np(a)
    top = np.concatenate([hi, lo], axis=1)
    bottom = np.concatenate([hi, np.zeros_like(hi)], axis=1)
    return np.concatenate([top, bottom], axis=0)


def constants():
    n = np.arange(1, N + 1, dtype=np.float64)
    q = math.sqrt(2.0 / (N + 1)) * np.sin(math.pi * n[:, None] * n[None, :] / (N + 1))
    e = 2.0 - 2.0 * np.cos(math.pi * n / (N + 1))
    tangent = np.diag(np.full(N, -2.0)) + np.diag(np.ones(N - 1), 1) + np.diag(np.ones(N - 1), -1)
    tangent[0, 0] = tangent[-1, -1] = -1.0
    smooth = np.eye(N) + penalty_mix * (q @ tangent @ q)
    half = N // 2
    sign = (-1.0) ** np.arange(half)
    fold = np.block([[q, q], [q, -q]])
    even, odd = q[0::2, :half], q[1::2, :half] * sign[None, :]
    lx = rows3(q)
    ly = rows3(np.concatenate([even, odd], axis=0))
    lyi = rows3(np.concatenate([even.T, odd.T], axis=0))
    wz = square3(fold)
    mx = square3(np.kron(np.eye(2), smooth))
    normal = q[0] + traction_mix * (11.0 / 6.0 * q[0] - 3.0 * q[1] + 1.5 * q[2] - q[3] / 3.0)
    table = np.stack([normal, q[0], e]).astype(np.float32)
    spread = lambda v: np.repeat(v.reshape(half, 2), N, axis=1)
    planes = np.stack(
        [spread(normal), spread(q[0]), spread(e) + np.tile(e, 2)[None, :]]
    ).astype(np.float32)
    return lx, ly, lyi, wz, mx, table, planes


def step_weights():
    mid = 0.5 * (upper_edge + lower_edge)
    radius = 0.5 * (upper_edge - lower_edge)
    return [
        1.0 / (mid + radius * math.cos(math.pi * (2 * k + 1) / (2 * ITERS))) for k in range(ITERS)
    ]


def lane_iota():
    return lax.broadcasted_iota(jnp.int32, (1, 128), 1)


def split(a):
    hi = a.astype(BF16)
    lo = (a - hi.astype(F32)).astype(BF16)
    return hi, lo


def stack3(a):
    hi, lo = split(a)
    return jnp.concatenate([hi, lo, hi], axis=0)


def times_square(a, w):
    hi, lo = split(a)
    r = jnp.dot(jnp.concatenate([hi, lo], axis=1), w, preferred_element_type=F32)
    return r[:, :128] + r[:, 128:]


def dot(a, b):
    return jnp.dot(a, b, preferred_element_type=F32)


def forward_zx(x_ref, t_ref, wz, lx, unroll):
    low = lane_iota() < N

    def body(p, carry):
        a = x_ref[:, pl.ds(pl.multiple_of(p * 128, 128), 128)]
        b = x_ref[:, pl.ds(pl.multiple_of((31 - p) * 128, 128), 128)]
        both = jnp.concatenate([jnp.where(low, a, b), jnp.where(low, b, a)], axis=0)
        z = times_square(both, wz)
        r = dot(lx, stack3(jnp.concatenate([z[:N], z[N:]], axis=1)))
        at = pl.multiple_of(p * 128, 128)
        t_ref[pl.ds(at, N), :] = r[:, :128]
        t_ref[pl.ds(at + N, N), :] = r[:, 128:]
        return carry

    lax.fori_loop(0, 16, body, 0, unroll=unroll)


def pair_y(ly, a, b):
    low = lane_iota() < N
    r = dot(ly, stack3(jnp.concatenate([a, b], axis=1)))
    return (
        jnp.where(low, r[:32, :128], r[32:, :128]),
        jnp.where(low, r[:32, 128:], r[32:, 128:]),
    )


def orient_row(code):
    lane = lane_iota()
    rows = jnp.where(lane < N, 1.0, -1.0)
    cols = jnp.where(lane % 2 == 0, 1.0, -1.0)
    one = jnp.ones((1, 128), F32)
    return jnp.where(code % 2 == 1, rows, one) * jnp.where(code // 2 == 1, cols, one)


def face_sums(se, so, y, m, g_ref, add):
    low = lane_iota() < N
    swapped = pltpu.roll(y, N, 1)
    total, diff = y + swapped, y - swapped
    parts = [
        se - so,
        se + so,
        jnp.where(low, diff[:32], -diff[32:]),
        jnp.where(low, total[:32], total[32:]),
    ]
    for at, part in enumerate(parts):
        rows = slice(32 * at, 32 * at + 32)
        value = m * part
        g_ref[rows, :] = value + g_ref[rows, :] if add else value


def spread_traces(lam, m, lx_ref, ly_ref):
    low = lane_iota() < N
    scale = inject_scale * m
    xh, xl, yh, yl = (lam[32 * i : 32 * i + 32] for i in range(4))
    lx_ref[0] = scale * (xl + xh)
    lx_ref[1] = scale * (xl - xh)
    pe, po = scale * (yl + yh), scale * (yl - yh)
    ly_ref[0:32, :] = jnp.where(low, pe, pltpu.roll(po, N, 1))
    ly_ref[32:64, :] = jnp.where(low, pltpu.roll(pe, N, 1), po)


def trace_kernel(
    f_hbm, mod, codes, table, lx_c, ly_c, wz_c, mx_c, planes,
    u_out, g_out, tx_out, ty_out,
    xin, t_scr, y_scr, face, lam, msend, mrecv, send, recv,
    in_sem, msend_sem, mrecv_sem, send_sem, recv_sem,
):
    s, j = lax.axis_index("blk"), lax.axis_index("face")
    ns, nj = lax.axis_size("blk"), lax.axis_size("face")
    partner = [
        (lax.rem(s + ns - 1, ns), j),
        (lax.rem(s + 1, ns), j),
        (s, lax.rem(j + nj - 1, nj)),
        (s, lax.rem(j + 1, nj)),
    ]
    barrier = pltpu.get_barrier_semaphore()
    loads = [pltpu.make_async_copy(f_hbm.at[c], xin.at[c], in_sem.at[c]) for c in range(COMPS)]
    for load in loads:
        load.start()
    for device in partner:
        pl.semaphore_signal(barrier, inc=1, device_id=device, device_id_type=MESH)

    row = lax.broadcasted_iota(jnp.int32, (8, 128), 0)
    moduli = [mod[0, 0, c] for c in range(COMPS)]
    msend[...] = jnp.where(row == 0, moduli[0], jnp.where(row == 1, moduli[1], moduli[2]))
    flip = orient_row(codes[0, 0])
    live_high = jnp.where(s < ns - 1, 1.0, 0.0).astype(F32)
    live_low = jnp.where(s > 0, 1.0, 0.0).astype(F32)
    omegas = step_weights()

    def fill(i, carry):
        ejk = planes[2]
        for c in range(COMPS):
            d = moduli[c] * (ejk + table[2, i]) + mass_shift
            r = pl.reciprocal(d, approx=True)
            g_out[c, i] = r * (2.0 - d * r)
        return carry

    lax.fori_loop(0, N, fill, 0, unroll=2)

    pl.semaphore_wait(barrier, 4)

    def mcopy(d):
        return pltpu.make_async_remote_copy(
            src_ref=msend, dst_ref=mrecv.at[d], send_sem=msend_sem.at[d],
            recv_sem=mrecv_sem.at[d], device_id=partner[d], device_id_type=MESH,
        )

    def gcopy(k, c, d):
        return pltpu.make_async_remote_copy(
            src_ref=send.at[k, c, d], dst_ref=recv.at[k, c, d], send_sem=send_sem.at[k, c, d],
            recv_sem=recv_sem.at[k, c, d], device_id=partner[d], device_id_type=MESH,
        )

    for d in range(4):
        mcopy(d).start()

    def send_faces(k, c):
        send[k, c, 0] = face[c, 32:64, :]
        send[k, c, 1] = face[c, 0:32, :] * flip
        send[k, c, 2] = face[c, 96:128, :]
        send[k, c, 3] = face[c, 64:96, :]
        for d in range(4):
            gcopy(k, c, d).start()

    def reduce_group(values, base, carry):
        se, so = carry
        cj = planes[0]
        sums = []
        for n, u in enumerate(values):
            weighted = table[0, base + n] * u
            if n % 2 == 0:
                se = se + weighted
            else:
                so = so + weighted
            w = cj * u
            sums.append((w[0:8] + w[8:16]) + (w[16:24] + w[24:32]))
        y = jnp.sum(jnp.stack(sums, axis=0), axis=1)
        y_scr[pl.ds(pl.multiple_of(base, 8), 8), :] = y
        return se, so

    zero = jnp.zeros((32, 128), F32)

    for c in range(COMPS):
        loads[c].wait()
        forward_zx(xin.at[c], t_scr, wz_c[...], lx_c[...], 2)

        def solve_group(group, carry, c=c):
            base = group * 8
            values = []
            for n in range(0, 8, 2):
                a = t_scr[pl.ds(base + n, 32, stride=N), :]
                b = t_scr[pl.ds(base + n + 1, 32, stride=N), :]
                for off, h in enumerate(pair_y(ly_c[...], a, b)):
                    u = h * g_out[c, base + n + off]
                    u_out[c, base + n + off] = u
                    values.append(u)
            return reduce_group(values, base, carry)

        se, so = lax.fori_loop(0, 8, solve_group, (zero, zero))
        face_sums(se, so, y_scr[...], moduli[c], face.at[c], False)
        send_faces(0, c)

    for d in range(4):
        mcopy(d).wait_recv()

    def update(k, c):
        for d in range(4):
            gcopy(k, c, d).wait_recv()
        m = moduli[c]
        order = [0, 1, 2, 3]
        residues = []
        for at, d in enumerate(order):
            other = recv[k, c, d]
            if d == 0:
                other = other * flip
            inverse = 1.0 / (m + mrecv[d, c : c + 1, :])
            r = (face[c, 32 * at : 32 * at + 32, :] + other) * inverse
            if k > 0:
                r = r - lam[c, 32 * at : 32 * at + 32, :]
            if d == 0:
                r = r * live_high
            if d == 1:
                r = r * live_low
            residues.append(r)
        step = omegas[k] * times_square(jnp.concatenate(residues, axis=0), mx_c[...])
        new = step + lam[c] if k > 0 else step
        lam[c] = new
        spread_traces(new, m, tx_out.at[c], ty_out.at[c])

    for c in range(COMPS):
        update(0, c)

        def move_group(group, carry, c=c):
            base = group * 8
            values = []
            q0j = planes[1]
            for n in range(8):
                i = base + n
                add = table[1, i] * tx_out[c, n % 2] + q0j * ty_out[c, pl.ds(i, 1), :]
                values.append(g_out[c, i] * add)
            return reduce_group(values, base, carry)

        se, so = lax.fori_loop(0, 8, move_group, (zero, zero))
        face_sums(se, so, y_scr[...], moduli[c], face.at[c], True)
        send_faces(1, c)

    for c in range(COMPS):
        update(1, c)
    for d in range(4):
        mcopy(d).wait_send()
    for k in range(ITERS):
        for c in range(COMPS):
            for d in range(4):
                gcopy(k, c, d).wait_send()


CHUNKS = 4


def back_kernel(u_ref, g_ref, tx, ty, table, lx_c, lyi_c, wz_c, planes, out_hbm, t_scr, o_scr, out_sem):
    low = lane_iota() < N

    def ocopy(c, chunk, side):
        first = chunk * 512 if side == 0 else 3584 - chunk * 512
        return pltpu.make_async_copy(
            o_scr.at[c, :, pl.ds(first, 512)],
            out_hbm.at[c, :, pl.ds(first, 512)],
            out_sem.at[c, chunk, side],
        )

    for c in range(COMPS):

        def solve_pair(pair, carry, c=c):
            q0j = planes[1]
            values = []
            for n in range(2):
                i = pair * 2 + n
                add = table[1, i] * tx[c, n] + q0j * ty[c, pl.ds(i, 1), :]
                values.append(u_ref[c, i] + g_ref[c, i] * add)
            a, b = pair_y(lyi_c[...], *values)
            t_scr[pl.ds(pair * 2, 32, stride=N), :] = a
            t_scr[pl.ds(pair * 2 + 1, 32, stride=N), :] = b
            return carry

        lax.fori_loop(0, 32, solve_pair, 0, unroll=4)

        def body(p, carry, c=c):
            at = pl.multiple_of(p * 128, 128)
            z = jnp.concatenate([t_scr[pl.ds(at, N), :], t_scr[pl.ds(at + N, N), :]], axis=1)
            r = dot(lx_c[...], stack3(z))
            o = times_square(jnp.concatenate([r[:, :128], r[:, 128:]], axis=0), wz_c[...])
            a, b = o[:N], o[N:]
            o_scr[c, :, pl.ds(at, 128)] = jnp.where(low, a, b)
            o_scr[c, :, pl.ds(pl.multiple_of((31 - p) * 128, 128), 128)] = jnp.where(low, b, a)
            return carry

        for chunk in range(CHUNKS):
            lax.fori_loop(4 * chunk, 4 * chunk + 4, body, 0, unroll=2)
            ocopy(c, chunk, 0).start()
            ocopy(c, chunk, 1).start()
    for c in range(COMPS):
        for chunk in range(CHUNKS):
            ocopy(c, chunk, 0).wait()
            ocopy(c, chunk, 1).wait()


def shards(forcing, modulus, orient_codes):
    lx, ly, lyi, wz, mx, table, planes = (jnp.asarray(a) for a in constants())
    f = forcing.reshape(COMPS, N, N * N)
    vmem = pl.BlockSpec(memory_space=pltpu.VMEM)
    smem = pl.BlockSpec(memory_space=pltpu.SMEM)
    hbm = pl.BlockSpec(memory_space=pltpu.HBM)
    spectral = (COMPS, N, N // 2, 128)
    shapes = [spectral, spectral, (COMPS, 2, 32, 128), (COMPS, N, 128)]
    u, g, tx, ty = pl.pallas_call(
        trace_kernel,
        out_shape=[pltpu.VMEM(shape, F32) for shape in shapes],
        in_specs=[hbm, smem, smem, smem, vmem, vmem, vmem, vmem, vmem],
        out_specs=[vmem] * 4,
        scratch_shapes=[
            pltpu.VMEM((COMPS, N, N * N), F32),
            pltpu.VMEM((32 * N, 128), F32),
            pltpu.VMEM((N, 128), F32),
            pltpu.VMEM((COMPS, 128, 128), F32),
            pltpu.VMEM((COMPS, 128, 128), F32),
            pltpu.VMEM((8, 128), F32),
            pltpu.VMEM((4, 8, 128), F32),
            pltpu.VMEM((ITERS, COMPS, 4, 32, 128), F32),
            pltpu.VMEM((ITERS, COMPS, 4, 32, 128), F32),
            pltpu.SemaphoreType.DMA((COMPS,)),
            pltpu.SemaphoreType.DMA((4,)),
            pltpu.SemaphoreType.DMA((4,)),
            pltpu.SemaphoreType.DMA((ITERS, COMPS, 4)),
            pltpu.SemaphoreType.DMA((ITERS, COMPS, 4)),
        ],
        compiler_params=pltpu.CompilerParams(
            collective_id=0, has_side_effects=True, vmem_limit_bytes=40 * 2**20
        ),
        cost_estimate=pl.CostEstimate(flops=2 * 10**9, bytes_accessed=3 * 2**20, transcendentals=0),
        name="traces",
    )(f, modulus, orient_codes, table, lx, ly, wz, mx, planes)
    out = pl.pallas_call(
        back_kernel,
        out_shape=jax.ShapeDtypeStruct((COMPS, N, N * N), F32),
        in_specs=[vmem] * 4 + [smem] + [vmem] * 4,
        out_specs=hbm,
        scratch_shapes=[
            pltpu.VMEM((32 * N, 128), F32),
            pltpu.VMEM((COMPS, N, N * N), F32),
            pltpu.SemaphoreType.DMA((COMPS, CHUNKS, 2)),
        ],
        compiler_params=pltpu.CompilerParams(vmem_limit_bytes=40 * 2**20),
        cost_estimate=pl.CostEstimate(flops=2 * 10**9, bytes_accessed=3 * 2**20, transcendentals=0),
        name="back",
    )(u, g, tx, ty, table, lx, lyi, wz, planes)
    return out.reshape(forcing.shape)


def solution(mesh):
    placed = (P("blk", "face", None, None, None), P("blk", "face", None), P("blk", "face"))
    return jax.shard_map(
        shards,
        mesh=mesh,
        in_specs=placed,
        out_specs=P("blk", "face", None, None, None),
        check_vma=False,
    )
```

profile of v0, /device:TPU:0, one launch (start us, length us, event | category | flops | bytes accessed | tf_op | source)
XLA Modules:
  0.0 58.4 jit_solution(9820032464426677668)
XLA Ops:
  0.7 0.0 copy-start
  0.7 0.9 %copy-done = bf16[256,256]{1,0:T(8,128)(2,1)S(1)} copy-done((bf16[256,256]{1,0:T(8,128)(2,1)S(1)}, bf16[256,256]{1,0:T(8,128)(2,1)}, u32[]{:S(2)}) %copy-start) | copy-done | bytes 131096
  1.6 0.0 copy-start.1
  1.6 0.8 %copy-done.1 = f32[3,32,128]{2,1,0:T(8,128)S(1)} copy-done((f32[3,32,128]{2,1,0:T(8,128)S(1)}, f32[3,32,128]{2,1,0:T(8,128)}, u32[]{:S(2)}) %copy-start.1) | copy-done | bytes 49176
  2.4 0.0 copy-start.2
  2.4 0.8 %copy-done.2 = bf16[64,192]{1,0:T(8,128)(2,1)S(1)} copy-done((bf16[64,192]{1,0:T(8,128)(2,1)S(1)}, bf16[64,192]{1,0:T(8,128)(2,1)}, u32[]{:S(2)}) %copy-start.2) | copy-done | bytes 24600
  3.1 0.0 copy-start.4
  3.1 0.7 %copy-done.4 = f32[3,64]{1,0:T(4,128)S(1)} copy-done((f32[3,64]{1,0:T(4,128)S(1)}, f32[3,64]{1,0:T(4,128)}, u32[]{:S(2)}) %copy-start.4) | copy-done | bytes 792
  3.8 0.0 copy-start.5
  3.8 1.9 %copy-done.5 = f32[1,1,3,64,4096]{4,3,2,1,0:T(8,128)S(1)} copy-done((f32[1,1,3,64,4096]{4,3,2,1,0:T(8,128)S(1)}, f32[1,1,3,64,4096]{4,3,2,1,0:T(8,128)}, u32[]{:S(2)}) %copy-start.5) | copy-done | bytes 3145752
  5.7 0.0 copy-start.6
  5.7 0.7 %copy-done.6 = f32[1,1,3]{2,1,0:T(1,128)S(1)} copy-done((f32[1,1,3]{2,1,0:T(1,128)S(1)}, f32[1,1,3]{2,1,0:T(1,128)}, u32[]{:S(2)}) %copy-start.6) | copy-done | bytes 36
  6.3 0.0 copy-start.7
  6.3 0.9 %copy-done.7 = bf16[256,256]{1,0:T(8,128)(2,1)S(1)} copy-done((bf16[256,256]{1,0:T(8,128)(2,1)S(1)}, bf16[256,256]{1,0:T(8,128)(2,1)}, u32[]{:S(2)}) %copy-start.7) | copy-done | bytes 131096
  7.2 0.0 copy-start.8
  7.3 0.7 %copy-done.8 = bf16[64,96]{1,0:T(8,128)(2,1)S(1)} copy-done((bf16[64,96]{1,0:T(8,128)(2,1)S(1)}, bf16[64,96]{1,0:T(8,128)(2,1)}, u32[]{:S(2)}) %copy-start.8) | copy-done | bytes 12312
  8.0 0.0 copy-start.3
  8.0 35.4 %traces.1 = (f32[3,64,32,128]{3,2,1,0:T(8,128)S(1)}, f32[3,64,32,128]{3,2,1,0:T(8,128)S(1)}, f32[3,2,32,128]{3,2,1,0:T(8,128)S(1)}, f32[3,64,128]{2,1,0:T(8,128)S(1)}) custom-call(f32[3,64,4096]{2,1,0:T(8,128)S(1)} %bitcast.2, f32[1,1,3]{2,1,0:T(1,128)S(1)} %copy-done.6, s32[1,1]{1,0:T(1,128)S(6)} %copy.11.codes, f32[3,64]{1,0:T(4,128)S(1)} %copy-done.4, ...), custom_call_target="tpu_custom_call" | custom-call | flops 2000000000 | bytes 3145728 | tf_op jit(solution)/shard_map/traces/pallas_call | solution.py:379
  43.4 0.0 copy-done.3
  43.4 15.0 %back.1 = f32[3,64,4096]{2,1,0:T(8,128)} custom-call(f32[3,64,32,128]{3,2,1,0:T(8,128)S(1)} %get-tuple-element.9.u_ref, f32[3,64,32,128]{3,2,1,0:T(8,128)S(1)} %get-tuple-element.10.g_ref, f32[3,2,32,128]{3,2,1,0:T(8,128)S(1)} %get-tuple-element.11.tx, f32[3,64,128]{2,1,0:T(8,128)S(1)} %get-tuple-element.12.ty, f32[3,64]{1,0:T(4,128)S(1)} %copy-done.4, ...), custom_call_target="tpu_custom_call" | custom-call | flops 2000000000 | bytes 3145728 | tf_op jit(solution)/shard_map/back/pallas_call | solution.py:406
Async XLA Ops:
  0.7 0.9 %copy-start = (bf16[256,256]{1,0:T(8,128)(2,1)S(1)}, bf16[256,256]{1,0:T(8,128)(2,1)}, u32[]{:S(2)}) copy-start(bf16[256,256]{1,0:T(8,128)(2,1)} %constant.17.clone.wz_c) | copy-start | bytes 393220
  1.6 0.8 %copy-start.1 = (f32[3,32,128]{2,1,0:T(8,128)S(1)}, f32[3,32,128]{2,1,0:T(8,128)}, u32[]{:S(2)}) copy-start(f32[3,32,128]{2,1,0:T(8,128)} %constant.20.clone.planes) | copy-start | bytes 147460
  2.4 0.8 %copy-start.2 = (bf16[64,192]{1,0:T(8,128)(2,1)S(1)}, bf16[64,192]{1,0:T(8,128)(2,1)}, u32[]{:S(2)}) copy-start(bf16[64,192]{1,0:T(8,128)(2,1)} %constant.14.clone.lx_c) | copy-start | bytes 73732
  3.1 0.7 %copy-start.4 = (f32[3,64]{1,0:T(4,128)S(1)}, f32[3,64]{1,0:T(4,128)}, u32[]{:S(2)}) copy-start(f32[3,64]{1,0:T(4,128)} %constant.19.clone.table) | copy-start | bytes 2308
  3.8 1.9 %copy-start.5 = (f32[1,1,3,64,4096]{4,3,2,1,0:T(8,128)S(1)}, f32[1,1,3,64,4096]{4,3,2,1,0:T(8,128)}, u32[]{:S(2)}) copy-start(f32[1,1,3,64,4096]{4,3,2,1,0:T(8,128)} %param.10) | copy-start | bytes 9437188
  5.7 0.7 %copy-start.6 = (f32[1,1,3]{2,1,0:T(1,128)S(1)}, f32[1,1,3]{2,1,0:T(1,128)}, u32[]{:S(2)}) copy-start(f32[1,1,3]{2,1,0:T(1,128)} %mod.1) | copy-start | bytes 40
  6.3 0.9 %copy-start.7 = (bf16[256,256]{1,0:T(8,128)(2,1)S(1)}, bf16[256,256]{1,0:T(8,128)(2,1)}, u32[]{:S(2)}) copy-start(bf16[256,256]{1,0:T(8,128)(2,1)} %constant.18.clone.mx_c) | copy-start | bytes 393220
  7.2 0.7 %copy-start.8 = (bf16[64,96]{1,0:T(8,128)(2,1)S(1)}, bf16[64,96]{1,0:T(8,128)(2,1)}, u32[]{:S(2)}) copy-start(bf16[64,96]{1,0:T(8,128)(2,1)} %constant.15.clone.ly_c) | copy-start | bytes 36868
  8.0 35.4 %copy-start.3 = (bf16[64,96]{1,0:T(8,128)(2,1)S(1)}, bf16[64,96]{1,0:T(8,128)(2,1)}, u32[]{:S(2)}) copy-start(bf16[64,96]{1,0:T(8,128)(2,1)} %constant.16.clone.lyi_c) | copy-start | bytes 36868
where the time goes:
time: 58.8 us; the launch traced here: 58.4 us
  Pallas kernels  50.4 us (86%)
  local copies, waits for them, and re-layouts  7.3 us (12%)
  between operations  0.68 us (1%)
    pallas_call x1, Pallas kernels, shards(): pl.pallas_call(trace_kernel, out_shape=[pltpu.VMEM(shape, F32) for shape...  35.4 us
    pallas_call x1, Pallas kernels, shards(): pl.pallas_call(back_kernel, out_shape=jax.ShapeDtypeStruct((COMPS, N, N *...  15 us
    unnamed x18, local copies, waits for them, and re-layouts  7.3 us

commit v1 on v0

--- a/solution.py
+++ b/solution.py
@@ -13,6 +13,7 @@
 N = 64
 ITERS = 2
 COMPS = 3
+STRIDE = 72
 MESH = pl.DeviceIdType.MESH
 F32 = jnp.float32
 BF16 = jnp.bfloat16
@@ -22,6 +23,10 @@
 penalty_mix = 0.25
 lower_edge = 0.3
 upper_edge = 1.5
+
+
+def in_hbm(a):
+    return pltpu.with_memory_space_constraint(a, pltpu.HBM)
 
 
 def split_np(a):
@@ -101,21 +106,35 @@
     return jnp.dot(a, b, preferred_element_type=F32)
 
 
-def forward_zx(x_ref, t_ref, wz, lx, unroll):
+def row_at(y):
+    return slice(y * STRIDE, y * STRIDE + N)
+
+
+def z_forward(x_ref, t_ref, wz):
     low = lane_iota() < N
-
-    def body(p, carry):
-        a = x_ref[:, pl.ds(pl.multiple_of(p * 128, 128), 128)]
-        b = x_ref[:, pl.ds(pl.multiple_of((31 - p) * 128, 128), 128)]
-        both = jnp.concatenate([jnp.where(low, a, b), jnp.where(low, b, a)], axis=0)
-        z = times_square(both, wz)
-        r = dot(lx, stack3(jnp.concatenate([z[:N], z[N:]], axis=1)))
-        at = pl.multiple_of(p * 128, 128)
-        t_ref[pl.ds(at, N), :] = r[:, :128]
-        t_ref[pl.ds(at + N, N), :] = r[:, 128:]
-        return carry
-
-    lax.fori_loop(0, 16, body, 0, unroll=unroll)
+    for p in range(16):
+        a = x_ref[:, p * 128 : p * 128 + 128]
+        b = x_ref[:, (31 - p) * 128 : (32 - p) * 128]
+        z = times_square(jnp.concatenate([jnp.where(low, a, b), jnp.where(low, b, a)], axis=0), wz)
+        t_ref[row_at(2 * p), :] = z[:N]
+        t_ref[row_at(2 * p + 1), :] = z[N:]
+
+
+def x_either(a_ref, b_ref, lx):
+    for p in range(16):
+        a = jnp.concatenate([a_ref[row_at(2 * p), :], a_ref[row_at(2 * p + 1), :]], axis=1)
+        r = dot(lx, stack3(a))
+        b_ref[row_at(2 * p), :] = r[:, :128]
+        b_ref[row_at(2 * p + 1), :] = r[:, 128:]
+
+
+def z_back(t_ref, o_ref, wz, p):
+    low = lane_iota() < N
+    both = jnp.concatenate([t_ref[row_at(2 * p), :], t_ref[row_at(2 * p + 1), :]], axis=0)
+    o = times_square(both, wz)
+    a, b = o[:N], o[N:]
+    o_ref[:, p * 128 : p * 128 + 128] = jnp.where(low, a, b)
+    o_ref[:, (31 - p) * 128 : (32 - p) * 128] = jnp.where(low, b, a)
 
 
 def pair_y(ly, a, b):
@@ -163,10 +182,10 @@
 
 
 def trace_kernel(
-    f_hbm, mod, codes, table, lx_c, ly_c, wz_c, mx_c, planes,
+    f_hbm, mod_h, codes, table_h, lx_h, ly_h, wz_h, mx_h, planes_h,
     u_out, g_out, tx_out, ty_out,
-    xin, t_scr, y_scr, face, lam, msend, mrecv, send, recv,
-    in_sem, msend_sem, mrecv_sem, send_sem, recv_sem,
+    mod, table, lx_c, ly_c, wz_c, mx_c, planes, xin, t_scr, x_scr, y_scr, face, lam, msend, mrecv, send, recv,
+    in_sem, con_sem, msend_sem, mrecv_sem, send_sem, recv_sem,
 ):
     s, j = lax.axis_index("blk"), lax.axis_index("face")
     ns, nj = lax.axis_size("blk"), lax.axis_size("face")
@@ -178,11 +197,23 @@
     ]
     barrier = pltpu.get_barrier_semaphore()
     loads = [pltpu.make_async_copy(f_hbm.at[c], xin.at[c], in_sem.at[c]) for c in range(COMPS)]
-    for load in loads:
+    pairs = [
+        (mod_h, mod), (table_h, table), (planes_h, planes),
+        (wz_h, wz_c), (lx_h, lx_c), (ly_h, ly_c), (mx_h, mx_c),
+    ]
+    small = [pltpu.make_async_copy(a, b, con_sem.at[i]) for i, (a, b) in enumerate(pairs)]
+    for copy in small[:3]:
+        copy.start()
+    loads[0].start()
+    for copy in small[3:]:
+        copy.start()
+    for load in loads[1:]:
         load.start()
     for device in partner:
         pl.semaphore_signal(barrier, inc=1, device_id=device, device_id_type=MESH)
 
+    for copy in small[:3]:
+        copy.wait()
     row = lax.broadcasted_iota(jnp.int32, (8, 128), 0)
     moduli = [mod[0, 0, c] for c in range(COMPS)]
     msend[...] = jnp.where(row == 0, moduli[0], jnp.where(row == 1, moduli[1], moduli[2]))
@@ -199,7 +230,7 @@
             g_out[c, i] = r * (2.0 - d * r)
         return carry
 
-    lax.fori_loop(0, N, fill, 0, unroll=2)
+    lax.fori_loop(0, N, fill, 0, unroll=4)
 
     pl.semaphore_wait(barrier, 4)
 
@@ -217,6 +248,8 @@
 
     for d in range(4):
         mcopy(d).start()
+    for copy in small[3:]:
+        copy.wait()
 
     def send_faces(k, c):
         send[k, c, 0] = face[c, 32:64, :]
@@ -239,33 +272,28 @@
             w = cj * u
             sums.append((w[0:8] + w[8:16]) + (w[16:24] + w[24:32]))
         y = jnp.sum(jnp.stack(sums, axis=0), axis=1)
-        y_scr[pl.ds(pl.multiple_of(base, 8), 8), :] = y
+        y_scr[base : base + 8, :] = y
         return se, so
 
     zero = jnp.zeros((32, 128), F32)
 
-    for c in range(COMPS):
+    def forward(c):
         loads[c].wait()
-        forward_zx(xin.at[c], t_scr, wz_c[...], lx_c[...], 2)
-
-        def solve_group(group, carry, c=c):
-            base = group * 8
+        z_forward(xin.at[c], t_scr, wz_c[...])
+        x_either(t_scr, x_scr, lx_c[...])
+        sums = (zero, zero)
+        for base in range(0, N, 8):
             values = []
             for n in range(0, 8, 2):
-                a = t_scr[pl.ds(base + n, 32, stride=N), :]
-                b = t_scr[pl.ds(base + n + 1, 32, stride=N), :]
+                a = x_scr[pl.ds(base + n, 32, stride=STRIDE), :]
+                b = x_scr[pl.ds(base + n + 1, 32, stride=STRIDE), :]
                 for off, h in enumerate(pair_y(ly_c[...], a, b)):
                     u = h * g_out[c, base + n + off]
                     u_out[c, base + n + off] = u
                     values.append(u)
-            return reduce_group(values, base, carry)
-
-        se, so = lax.fori_loop(0, 8, solve_group, (zero, zero))
-        face_sums(se, so, y_scr[...], moduli[c], face.at[c], False)
+            sums = reduce_group(values, base, sums)
+        face_sums(*sums, y_scr[...], moduli[c], face.at[c], False)
         send_faces(0, c)
-
-    for d in range(4):
-        mcopy(d).wait_recv()
 
     def update(k, c):
         for d in range(4):
@@ -291,23 +319,27 @@
         lam[c] = new
         spread_traces(new, m, tx_out.at[c], ty_out.at[c])
 
-    for c in range(COMPS):
+    def move(c):
         update(0, c)
-
-        def move_group(group, carry, c=c):
-            base = group * 8
+        sums = (zero, zero)
+        q0j = planes[1]
+        for base in range(0, N, 8):
             values = []
-            q0j = planes[1]
-            for n in range(8):
-                i = base + n
-                add = table[1, i] * tx_out[c, n % 2] + q0j * ty_out[c, pl.ds(i, 1), :]
+            for i in range(base, base + 8):
+                add = table[1, i] * tx_out[c, i % 2] + q0j * ty_out[c, i : i + 1, :]
                 values.append(g_out[c, i] * add)
-            return reduce_group(values, base, carry)
-
-        se, so = lax.fori_loop(0, 8, move_group, (zero, zero))
-        face_sums(se, so, y_scr[...], moduli[c], face.at[c], True)
+            sums = reduce_group(values, base, sums)
+        face_sums(*sums, y_scr[...], moduli[c], face.at[c], True)
         send_faces(1, c)
 
+    forward(0)
+    forward(1)
+    for d in range(4):
+        mcopy(d).wait_recv()
+    move(0)
+    forward(2)
+    move(1)
+    move(2)
     for c in range(COMPS):
         update(1, c)
     for d in range(4):
@@ -321,8 +353,7 @@
 CHUNKS = 4
 
 
-def back_kernel(u_ref, g_ref, tx, ty, table, lx_c, lyi_c, wz_c, planes, out_hbm, t_scr, o_scr, out_sem):
-    low = lane_iota() < N
+def back_kernel(u_ref, g_ref, tx, ty, table, lx_c, lyi_c, wz_c, planes, out_hbm, t_scr, x_scr, o_scr, out_sem):
 
     def ocopy(c, chunk, side):
         first = chunk * 512 if side == 0 else 3584 - chunk * 512
@@ -333,33 +364,19 @@
         )
 
     for c in range(COMPS):
-
-        def solve_pair(pair, carry, c=c):
-            q0j = planes[1]
+        q0j = planes[1]
+        for i in range(0, N, 2):
             values = []
             for n in range(2):
-                i = pair * 2 + n
-                add = table[1, i] * tx[c, n] + q0j * ty[c, pl.ds(i, 1), :]
-                values.append(u_ref[c, i] + g_ref[c, i] * add)
+                add = table[1, i + n] * tx[c, n] + q0j * ty[c, i + n : i + n + 1, :]
+                values.append(u_ref[c, i + n] + g_ref[c, i + n] * add)
             a, b = pair_y(lyi_c[...], *values)
-            t_scr[pl.ds(pair * 2, 32, stride=N), :] = a
-            t_scr[pl.ds(pair * 2 + 1, 32, stride=N), :] = b
-            return carry
-
-        lax.fori_loop(0, 32, solve_pair, 0, unroll=4)
-
-        def body(p, carry, c=c):
-            at = pl.multiple_of(p * 128, 128)
-            z = jnp.concatenate([t_scr[pl.ds(at, N), :], t_scr[pl.ds(at + N, N), :]], axis=1)
-            r = dot(lx_c[...], stack3(z))
-            o = times_square(jnp.concatenate([r[:, :128], r[:, 128:]], axis=0), wz_c[...])
-            a, b = o[:N], o[N:]
-            o_scr[c, :, pl.ds(at, 128)] = jnp.where(low, a, b)
-            o_scr[c, :, pl.ds(pl.multiple_of((31 - p) * 128, 128), 128)] = jnp.where(low, b, a)
-            return carry
-
+            t_scr[pl.ds(i, 32, stride=STRIDE), :] = a
+            t_scr[pl.ds(i + 1, 32, stride=STRIDE), :] = b
+        x_either(t_scr, x_scr, lx_c[...])
         for chunk in range(CHUNKS):
-            lax.fori_loop(4 * chunk, 4 * chunk + 4, body, 0, unroll=2)
+            for p in range(4 * chunk, 4 * chunk + 4):
+                z_back(x_scr, o_scr.at[c], wz_c[...], p)
             ocopy(c, chunk, 0).start()
             ocopy(c, chunk, 1).start()
     for c in range(COMPS):
@@ -379,11 +396,19 @@
     u, g, tx, ty = pl.pallas_call(
         trace_kernel,
         out_shape=[pltpu.VMEM(shape, F32) for shape in shapes],
-        in_specs=[hbm, smem, smem, smem, vmem, vmem, vmem, vmem, vmem],
+        in_specs=[hbm, hbm, smem] + [hbm] * 6,
         out_specs=[vmem] * 4,
         scratch_shapes=[
+            pltpu.SMEM((1, 1, COMPS), F32),
+            pltpu.SMEM(table.shape, F32),
+            pltpu.VMEM(lx.shape, BF16),
+            pltpu.VMEM(ly.shape, BF16),
+            pltpu.VMEM(wz.shape, BF16),
+            pltpu.VMEM(mx.shape, BF16),
+            pltpu.VMEM(planes.shape, F32),
             pltpu.VMEM((COMPS, N, N * N), F32),
-            pltpu.VMEM((32 * N, 128), F32),
+            pltpu.VMEM((32 * STRIDE, 128), F32),
+            pltpu.VMEM((32 * STRIDE, 128), F32),
             pltpu.VMEM((N, 128), F32),
             pltpu.VMEM((COMPS, 128, 128), F32),
             pltpu.VMEM((COMPS, 128, 128), F32),
@@ -392,6 +417,7 @@
             pltpu.VMEM((ITERS, COMPS, 4, 32, 128), F32),
             pltpu.VMEM((ITERS, COMPS, 4, 32, 128), F32),
             pltpu.SemaphoreType.DMA((COMPS,)),
+            pltpu.SemaphoreType.DMA((7,)),
             pltpu.SemaphoreType.DMA((4,)),
             pltpu.SemaphoreType.DMA((4,)),
             pltpu.SemaphoreType.DMA((ITERS, COMPS, 4)),
@@ -402,14 +428,15 @@
         ),
         cost_estimate=pl.CostEstimate(flops=2 * 10**9, bytes_accessed=3 * 2**20, transcendentals=0),
         name="traces",
-    )(f, modulus, orient_codes, table, lx, ly, wz, mx, planes)
+    )(in_hbm(f), in_hbm(modulus), orient_codes, *(in_hbm(a) for a in (table, lx, ly, wz, mx, planes)))
     out = pl.pallas_call(
         back_kernel,
         out_shape=jax.ShapeDtypeStruct((COMPS, N, N * N), F32),
         in_specs=[vmem] * 4 + [smem] + [vmem] * 4,
         out_specs=hbm,
         scratch_shapes=[
-            pltpu.VMEM((32 * N, 128), F32),
+            pltpu.VMEM((32 * STRIDE, 128), F32),
+            pltpu.VMEM((32 * STRIDE, 128), F32),
             pltpu.VMEM((COMPS, N, N * N), F32),
             pltpu.SemaphoreType.DMA((COMPS, CHUNKS, 2)),
         ],

time: 58.8 us -> 29.4 us (0.50)
  Pallas kernels: 50.4 us -> 28.5 us
  local copies, waits for them, and re-layouts: 7.3 us -> 0.03 us
    pallas_call x1, Pallas kernels: 35.4 us -> 23.4 us  [shards(): pl.pallas_call(trace_kernel, out_shape=[pltpu.VMEM(shape, F32) for shape...]
    pallas_call x1, Pallas kernels: 15 us -> 5.07 us  [shards(): pl.pallas_call(back_kernel, out_shape=jax.ShapeDtypeStruct((COMPS, N, N *...]
    unnamed x18 -> x10, local copies, waits for them, and re-layouts: 7.3 us -> 0.03 us
where the time goes in v1:
time: 29.4 us; the launch traced here: 29.3 us
  Pallas kernels  28.5 us (97%)
  between operations  0.74 us (3%)
    pallas_call x1, Pallas kernels, shards(): pl.pallas_call(trace_kernel, out_shape=[pltpu.VMEM(shape, F32) for shape...  23.4 us
    pallas_call x1, Pallas kernels, shards(): pl.pallas_call(back_kernel, out_shape=jax.ShapeDtypeStruct((COMPS, N, N *...  5.07 us

profile of v1, /device:TPU:0, one launch (start us, length us, event | category | flops | bytes accessed | tf_op | source)
XLA Modules:
  0.0 29.3 jit_solution(3553838044837038955)
XLA Ops:
  0.7 0.0 copy-start
  0.7 0.0 copy-start.1
  0.7 0.0 copy-start.2
  0.7 0.0 copy-start.3
  0.7 0.0 copy-start.4
  0.7 23.4 %traces.1 = (f32[3,64,32,128]{3,2,1,0:T(8,128)S(1)}, f32[3,64,32,128]{3,2,1,0:T(8,128)S(1)}, f32[3,2,32,128]{3,2,1,0:T(8,128)S(1)}, f32[3,64,128]{2,1,0:T(8,128)S(1)}) custom-call(f32[3,64,4096]{2,1,0:T(8,128)} %bitcast.2, f32[1,1,3]{2,1,0:T(1,128)} %mod_h.1, s32[1,1]{1,0:T(1,128)S(6)} %copy.11.codes, f32[3,64]{1,0:T(4,128)} %constant.19.clone.table_h.table, ...), custom_call_target="tpu_custom_call" | custom-call | flops 2000000000 | bytes 3145728 | tf_op jit(solution)/shard_map/traces/pallas_call | solution.py:396
  24.1 0.0 copy-done
  24.1 0.0 copy-done.1
  24.2 0.0 copy-done.2
  24.2 0.0 copy-done.3
  24.2 0.0 copy-done.4
  24.2 5.1 %back.1 = f32[3,64,4096]{2,1,0:T(8,128)} custom-call(f32[3,64,32,128]{3,2,1,0:T(8,128)S(1)} %get-tuple-element.9.u_ref, f32[3,64,32,128]{3,2,1,0:T(8,128)S(1)} %get-tuple-element.10.g_ref, f32[3,2,32,128]{3,2,1,0:T(8,128)S(1)} %get-tuple-element.11.tx, f32[3,64,128]{2,1,0:T(8,128)S(1)} %get-tuple-element.12.ty, f32[3,64]{1,0:T(4,128)S(1)} %copy-done.4, ...), custom_call_target="tpu_custom_call" | custom-call | flops 2000000000 | bytes 3145728 | tf_op jit(solution)/shard_map/back/pallas_call | solution.py:432
Async XLA Ops:
  0.7 23.5 %copy-start = (bf16[256,256]{1,0:T(8,128)(2,1)S(1)}, bf16[256,256]{1,0:T(8,128)(2,1)}, u32[]{:S(2)}) copy-start(bf16[256,256]{1,0:T(8,128)(2,1)} %constant.17.clone.wz_h.wz_c) | copy-start | bytes 393220
  0.7 23.5 %copy-start.1 = (f32[3,32,128]{2,1,0:T(8,128)S(1)}, f32[3,32,128]{2,1,0:T(8,128)}, u32[]{:S(2)}) copy-start(f32[3,32,128]{2,1,0:T(8,128)} %constant.20.clone.planes_h.planes) | copy-start | bytes 147460
  0.7 23.5 %copy-start.2 = (bf16[64,192]{1,0:T(8,128)(2,1)S(1)}, bf16[64,192]{1,0:T(8,128)(2,1)}, u32[]{:S(2)}) copy-start(bf16[64,192]{1,0:T(8,128)(2,1)} %constant.14.clone.lx_h.lx_c) | copy-start | bytes 73732
  0.7 23.5 %copy-start.3 = (bf16[64,96]{1,0:T(8,128)(2,1)S(1)}, bf16[64,96]{1,0:T(8,128)(2,1)}, u32[]{:S(2)}) copy-start(bf16[64,96]{1,0:T(8,128)(2,1)} %constant.16.clone.lyi_c) | copy-start | bytes 36868
  0.7 23.5 %copy-start.4 = (f32[3,64]{1,0:T(4,128)S(1)}, f32[3,64]{1,0:T(4,128)}, u32[]{:S(2)}) copy-start(f32[3,64]{1,0:T(4,128)} %constant.19.clone.table_h.table) | copy-start | bytes 2308

commit v2 on v1

--- a/solution.py
+++ b/solution.py
@@ -110,9 +110,9 @@
     return slice(y * STRIDE, y * STRIDE + N)
 
 
-def z_forward(x_ref, t_ref, wz):
+def z_forward(x_ref, t_ref, wz, steps):
     low = lane_iota() < N
-    for p in range(16):
+    for p in steps:
         a = x_ref[:, p * 128 : p * 128 + 128]
         b = x_ref[:, (31 - p) * 128 : (32 - p) * 128]
         z = times_square(jnp.concatenate([jnp.where(low, a, b), jnp.where(low, b, a)], axis=0), wz)
@@ -182,9 +182,10 @@
 
 
 def trace_kernel(
-    f_hbm, mod_h, codes, table_h, lx_h, ly_h, wz_h, mx_h, planes_h,
-    u_out, g_out, tx_out, ty_out,
-    mod, table, lx_c, ly_c, wz_c, mx_c, planes, xin, t_scr, x_scr, y_scr, face, lam, msend, mrecv, send, recv,
+    f_hbm, mod_h, codes, table_h, lx_h, ly_h, lyi_h, wz_h, mx_h, planes_h,
+    x_out,
+    mod, table, lx_c, ly_c, lyi_c, wz_c, mx_c, planes, u_out, g_out, tx_out, ty_out,
+    xin, t_scr, x_scr, y_scr, face, lam, msend, mrecv, send, recv,
     in_sem, con_sem, msend_sem, mrecv_sem, send_sem, recv_sem,
 ):
     s, j = lax.axis_index("blk"), lax.axis_index("face")
@@ -196,21 +197,52 @@
         (s, lax.rem(j + 1, nj)),
     ]
     barrier = pltpu.get_barrier_semaphore()
-    loads = [pltpu.make_async_copy(f_hbm.at[c], xin.at[c], in_sem.at[c]) for c in range(COMPS)]
+    strips = [
+        pltpu.make_async_copy(
+            f_hbm.at[0, :, pl.ds(at * 1024, 1024)], xin.at[0, :, pl.ds(at * 1024, 1024)],
+            in_sem.at[n],
+        )
+        for n, at in enumerate((0, 3, 1, 2))
+    ]
+    loads = [
+        pltpu.make_async_copy(f_hbm.at[c], xin.at[c], in_sem.at[3 + c]) for c in range(1, COMPS)
+    ]
     pairs = [
         (mod_h, mod), (table_h, table), (planes_h, planes),
-        (wz_h, wz_c), (lx_h, lx_c), (ly_h, ly_c), (mx_h, mx_c),
+        (wz_h, wz_c), (lx_h, lx_c), (ly_h, ly_c), (mx_h, mx_c), (lyi_h, lyi_c),
     ]
     small = [pltpu.make_async_copy(a, b, con_sem.at[i]) for i, (a, b) in enumerate(pairs)]
     for copy in small[:3]:
         copy.start()
-    loads[0].start()
-    for copy in small[3:]:
+    strips[0].start()
+    strips[1].start()
+    small[3].start()
+    strips[2].start()
+    strips[3].start()
+    for copy in small[4:]:
         copy.start()
-    for load in loads[1:]:
+    for load in loads:
         load.start()
-    for device in partner:
-        pl.semaphore_signal(barrier, inc=1, device_id=device, device_id_type=MESH)
+    recv[:, :, 0:2] = jnp.zeros((ITERS, COMPS, 2, 32, 128), F32)
+    mrecv[0:2] = jnp.ones((2, 8, 128), F32)
+    present = [s > 0, s < ns - 1, None, None]
+
+    def where_present(d, action):
+        if present[d] is None:
+            action()
+        else:
+            pl.when(present[d])(action)
+
+    def from_present(d, action):
+        where_present(d ^ 1 if d < 2 else d, action)
+
+    for d in range(4):
+        where_present(
+            d,
+            lambda d=d: pl.semaphore_signal(
+                barrier, inc=1, device_id=partner[d], device_id_type=MESH
+            ),
+        )
 
     for copy in small[:3]:
         copy.wait()
@@ -232,8 +264,6 @@
 
     lax.fori_loop(0, N, fill, 0, unroll=4)
 
-    pl.semaphore_wait(barrier, 4)
-
     def mcopy(d):
         return pltpu.make_async_remote_copy(
             src_ref=msend, dst_ref=mrecv.at[d], send_sem=msend_sem.at[d],
@@ -246,10 +276,6 @@
             recv_sem=recv_sem.at[k, c, d], device_id=partner[d], device_id_type=MESH,
         )
 
-    for d in range(4):
-        mcopy(d).start()
-    for copy in small[3:]:
-        copy.wait()
 
     def send_faces(k, c):
         send[k, c, 0] = face[c, 32:64, :]
@@ -257,7 +283,7 @@
         send[k, c, 2] = face[c, 96:128, :]
         send[k, c, 3] = face[c, 64:96, :]
         for d in range(4):
-            gcopy(k, c, d).start()
+            where_present(d, gcopy(k, c, d).start)
 
     def reduce_group(values, base, carry):
         se, so = carry
@@ -278,8 +304,19 @@
     zero = jnp.zeros((32, 128), F32)
 
     def forward(c):
-        loads[c].wait()
-        z_forward(xin.at[c], t_scr, wz_c[...])
+        if c == 0:
+            small[3].wait()
+            strips[0].wait()
+            strips[1].wait()
+            z_forward(xin.at[c], t_scr, wz_c[...], range(8))
+            strips[2].wait()
+            strips[3].wait()
+            z_forward(xin.at[c], t_scr, wz_c[...], range(8, 16))
+            for copy in small[4:]:
+                copy.wait()
+        else:
+            loads[c - 1].wait()
+            z_forward(xin.at[c], t_scr, wz_c[...], range(16))
         x_either(t_scr, x_scr, lx_c[...])
         sums = (zero, zero)
         for base in range(0, N, 8):
@@ -293,11 +330,15 @@
                     values.append(u)
             sums = reduce_group(values, base, sums)
         face_sums(*sums, y_scr[...], moduli[c], face.at[c], False)
+        if c == 0:
+            pl.semaphore_wait(barrier, 4 - jnp.where(s > 0, 0, 1) - jnp.where(s < ns - 1, 0, 1))
+            for d in range(4):
+                where_present(d, mcopy(d).start)
         send_faces(0, c)
 
     def update(k, c):
         for d in range(4):
-            gcopy(k, c, d).wait_recv()
+            from_present(d, gcopy(k, c, d).wait_recv)
         m = moduli[c]
         order = [0, 1, 2, 3]
         residues = []
@@ -332,29 +373,39 @@
         face_sums(*sums, y_scr[...], moduli[c], face.at[c], True)
         send_faces(1, c)
 
-    forward(0)
-    forward(1)
+    def back(c):
+        update(1, c)
+        q0j = planes[1]
+        for i in range(0, N, 2):
+            values = []
+            for n in range(2):
+                add = table[1, i + n] * tx_out[c, n] + q0j * ty_out[c, i + n : i + n + 1, :]
+                values.append(u_out[c, i + n] + g_out[c, i + n] * add)
+            a, b = pair_y(lyi_c[...], *values)
+            t_scr[pl.ds(i, 32, stride=STRIDE), :] = a
+            t_scr[pl.ds(i + 1, 32, stride=STRIDE), :] = b
+        x_either(t_scr, x_out.at[c], lx_c[...])
+
+    for c in range(COMPS):
+        forward(c)
     for d in range(4):
-        mcopy(d).wait_recv()
-    move(0)
-    forward(2)
-    move(1)
-    move(2)
+        from_present(d, mcopy(d).wait_recv)
     for c in range(COMPS):
-        update(1, c)
+        move(c)
+    for c in range(COMPS):
+        back(c)
     for d in range(4):
-        mcopy(d).wait_send()
+        where_present(d, mcopy(d).wait_send)
     for k in range(ITERS):
         for c in range(COMPS):
             for d in range(4):
-                gcopy(k, c, d).wait_send()
+                where_present(d, gcopy(k, c, d).wait_send)
 
 
 CHUNKS = 4
 
 
-def back_kernel(u_ref, g_ref, tx, ty, table, lx_c, lyi_c, wz_c, planes, out_hbm, t_scr, x_scr, o_scr, out_sem):
-
+def back_kernel(x_ref, wz_c, out_hbm, o_scr, out_sem):
     def ocopy(c, chunk, side):
         first = chunk * 512 if side == 0 else 3584 - chunk * 512
         return pltpu.make_async_copy(
@@ -364,19 +415,9 @@
         )
 
     for c in range(COMPS):
-        q0j = planes[1]
-        for i in range(0, N, 2):
-            values = []
-            for n in range(2):
-                add = table[1, i + n] * tx[c, n] + q0j * ty[c, i + n : i + n + 1, :]
-                values.append(u_ref[c, i + n] + g_ref[c, i + n] * add)
-            a, b = pair_y(lyi_c[...], *values)
-            t_scr[pl.ds(i, 32, stride=STRIDE), :] = a
-            t_scr[pl.ds(i + 1, 32, stride=STRIDE), :] = b
-        x_either(t_scr, x_scr, lx_c[...])
         for chunk in range(CHUNKS):
             for p in range(4 * chunk, 4 * chunk + 4):
-                z_back(x_scr, o_scr.at[c], wz_c[...], p)
+                z_back(x_ref.at[c], o_scr.at[c], wz_c[...], p)
             ocopy(c, chunk, 0).start()
             ocopy(c, chunk, 1).start()
     for c in range(COMPS):
@@ -392,20 +433,24 @@
     smem = pl.BlockSpec(memory_space=pltpu.SMEM)
     hbm = pl.BlockSpec(memory_space=pltpu.HBM)
     spectral = (COMPS, N, N // 2, 128)
-    shapes = [spectral, spectral, (COMPS, 2, 32, 128), (COMPS, N, 128)]
-    u, g, tx, ty = pl.pallas_call(
+    x_back = pl.pallas_call(
         trace_kernel,
-        out_shape=[pltpu.VMEM(shape, F32) for shape in shapes],
-        in_specs=[hbm, hbm, smem] + [hbm] * 6,
-        out_specs=[vmem] * 4,
+        out_shape=pltpu.VMEM((COMPS, 32 * STRIDE, 128), F32),
+        in_specs=[hbm, hbm, smem] + [hbm] * 7,
+        out_specs=vmem,
         scratch_shapes=[
             pltpu.SMEM((1, 1, COMPS), F32),
             pltpu.SMEM(table.shape, F32),
             pltpu.VMEM(lx.shape, BF16),
             pltpu.VMEM(ly.shape, BF16),
+            pltpu.VMEM(lyi.shape, BF16),
             pltpu.VMEM(wz.shape, BF16),
             pltpu.VMEM(mx.shape, BF16),
             pltpu.VMEM(planes.shape, F32),
+            pltpu.VMEM(spectral, F32),
+            pltpu.VMEM(spectral, F32),
+            pltpu.VMEM((COMPS, 2, 32, 128), F32),
+            pltpu.VMEM((COMPS, N, 128), F32),
             pltpu.VMEM((COMPS, N, N * N), F32),
             pltpu.VMEM((32 * STRIDE, 128), F32),
             pltpu.VMEM((32 * STRIDE, 128), F32),
@@ -416,8 +461,8 @@
             pltpu.VMEM((4, 8, 128), F32),
             pltpu.VMEM((ITERS, COMPS, 4, 32, 128), F32),
             pltpu.VMEM((ITERS, COMPS, 4, 32, 128), F32),
-            pltpu.SemaphoreType.DMA((COMPS,)),
-            pltpu.SemaphoreType.DMA((7,)),
+            pltpu.SemaphoreType.DMA((6,)),
+            pltpu.SemaphoreType.DMA((8,)),
             pltpu.SemaphoreType.DMA((4,)),
             pltpu.SemaphoreType.DMA((4,)),
             pltpu.SemaphoreType.DMA((ITERS, COMPS, 4)),
@@ -428,22 +473,20 @@
         ),
         cost_estimate=pl.CostEstimate(flops=2 * 10**9, bytes_accessed=3 * 2**20, transcendentals=0),
         name="traces",
-    )(in_hbm(f), in_hbm(modulus), orient_codes, *(in_hbm(a) for a in (table, lx, ly, wz, mx, planes)))
+    )(in_hbm(f), in_hbm(modulus), orient_codes, *(in_hbm(a) for a in (table, lx, ly, lyi, wz, mx, planes)))
     out = pl.pallas_call(
         back_kernel,
         out_shape=jax.ShapeDtypeStruct((COMPS, N, N * N), F32),
-        in_specs=[vmem] * 4 + [smem] + [vmem] * 4,
+        in_specs=[vmem] * 2,
         out_specs=hbm,
         scratch_shapes=[
-            pltpu.VMEM((32 * STRIDE, 128), F32),
-            pltpu.VMEM((32 * STRIDE, 128), F32),
             pltpu.VMEM((COMPS, N, N * N), F32),
             pltpu.SemaphoreType.DMA((COMPS, CHUNKS, 2)),
         ],
         compiler_params=pltpu.CompilerParams(vmem_limit_bytes=40 * 2**20),
         cost_estimate=pl.CostEstimate(flops=2 * 10**9, bytes_accessed=3 * 2**20, transcendentals=0),
         name="back",
-    )(u, g, tx, ty, table, lx, lyi, wz, planes)
+    )(x_back, wz)
     return out.reshape(forcing.shape)
 
 

time: 29.4 us -> 21.1 us (0.72)
  the two profiles are of different devices: /device:TPU:0 before, /device:TPU:24 now
where the time goes in v2:
time: 21.1 us; the launch traced here: 20.9 us
  Pallas kernels  20.3 us (96%)
  between operations  0.68 us (3%)
    pallas_call x1, Pallas kernels, shards(): pl.pallas_call(trace_kernel, out_shape=pltpu.VMEM((COMPS, 32 * STRIDE, 12...  18.2 us
    pallas_call x1, Pallas kernels, shards(): pl.pallas_call(back_kernel, out_shape=jax.ShapeDtypeStruct((COMPS, N, N *...  2.1 us

profile of v2, /device:TPU:24, one launch (start us, length us, event | category | flops | bytes accessed | tf_op | source)
XLA Modules:
  0.0 20.9 jit_solution(13944530061127746080)
XLA Ops:
  0.7 0.0 copy-start
  0.7 18.2 %traces.1.x_ref = f32[3,2304,128]{2,1,0:T(8,128)S(1)} custom-call(f32[3,64,4096]{2,1,0:T(8,128)} %bitcast.2, f32[1,1,3]{2,1,0:T(1,128)} %mod_h.1, s32[1,1]{1,0:T(1,128)S(6)} %copy.11.codes, f32[3,64]{1,0:T(4,128)} %constant.19.clone.table_h, bf16[64,192]{1,0:T(8,128)(2,1)} %constant.14.clone.lx_h, bf16[64,96]{1,0:T(8,128)(2,1)} %constant.15.clone.ly_h, ...), custom_call_target="tpu_custom_call" | custom-call | flops 2000000000 | bytes 3145728 | tf_op jit(solution)/shard_map/traces/pallas_call | solution.py:436
  18.8 0.0 copy-done
  18.8 2.1 %back.1 = f32[3,64,4096]{2,1,0:T(8,128)} custom-call(f32[3,2304,128]{2,1,0:T(8,128)S(1)} %traces.1.x_ref, bf16[256,256]{1,0:T(8,128)(2,1)S(1)} %copy-done), custom_call_target="tpu_custom_call" | custom-call | flops 2000000000 | bytes 3145728 | tf_op jit(solution)/shard_map/back/pallas_call | solution.py:477
Async XLA Ops:
  0.7 18.2 %copy-start = (bf16[256,256]{1,0:T(8,128)(2,1)S(1)}, bf16[256,256]{1,0:T(8,128)(2,1)}, u32[]{:S(2)}) copy-start(bf16[256,256]{1,0:T(8,128)(2,1)} %constant.17.clone.wz_h.wz_c) | copy-start | bytes 393220

commit v3 on v2

--- a/solution.py
+++ b/solution.py
@@ -183,7 +183,7 @@
 
 def trace_kernel(
     f_hbm, mod_h, codes, table_h, lx_h, ly_h, lyi_h, wz_h, mx_h, planes_h,
-    x_out,
+    y_out,
     mod, table, lx_c, ly_c, lyi_c, wz_c, mx_c, planes, u_out, g_out, tx_out, ty_out,
     xin, t_scr, x_scr, y_scr, face, lam, msend, mrecv, send, recv,
     in_sem, con_sem, msend_sem, mrecv_sem, send_sem, recv_sem,
@@ -212,11 +212,10 @@
         (wz_h, wz_c), (lx_h, lx_c), (ly_h, ly_c), (mx_h, mx_c), (lyi_h, lyi_c),
     ]
     small = [pltpu.make_async_copy(a, b, con_sem.at[i]) for i, (a, b) in enumerate(pairs)]
-    for copy in small[:3]:
-        copy.start()
     strips[0].start()
     strips[1].start()
-    small[3].start()
+    for copy in small[:4]:
+        copy.start()
     strips[2].start()
     strips[3].start()
     for copy in small[4:]:
@@ -254,15 +253,16 @@
     live_low = jnp.where(s > 0, 1.0, 0.0).astype(F32)
     omegas = step_weights()
 
+    def gain(c, i):
+        d = (moduli[c] * planes[2] + mass_shift) + moduli[c] * table[2, i]
+        r = pl.reciprocal(d, approx=True)
+        return r * (2.0 - d * r)
+
     def fill(i, carry):
-        ejk = planes[2]
-        for c in range(COMPS):
-            d = moduli[c] * (ejk + table[2, i]) + mass_shift
-            r = pl.reciprocal(d, approx=True)
-            g_out[c, i] = r * (2.0 - d * r)
+        g_out[0, i] = gain(0, i)
         return carry
 
-    lax.fori_loop(0, N, fill, 0, unroll=4)
+    lax.fori_loop(0, N, fill, 0, unroll=8)
 
     def mcopy(d):
         return pltpu.make_async_remote_copy(
@@ -325,8 +325,11 @@
                 a = x_scr[pl.ds(base + n, 32, stride=STRIDE), :]
                 b = x_scr[pl.ds(base + n + 1, 32, stride=STRIDE), :]
                 for off, h in enumerate(pair_y(ly_c[...], a, b)):
-                    u = h * g_out[c, base + n + off]
-                    u_out[c, base + n + off] = u
+                    i = base + n + off
+                    if c > 0:
+                        g_out[c, i] = gain(c, i)
+                    u = h * g_out[c, i]
+                    u_out[c, i] = u
                     values.append(u)
             sums = reduce_group(values, base, sums)
         face_sums(*sums, y_scr[...], moduli[c], face.at[c], False)
@@ -336,9 +339,11 @@
                 where_present(d, mcopy(d).start)
         send_faces(0, c)
 
-    def update(k, c):
+    def arrived(k, c):
         for d in range(4):
             from_present(d, gcopy(k, c, d).wait_recv)
+
+    def update(k, c):
         m = moduli[c]
         order = [0, 1, 2, 3]
         residues = []
@@ -361,6 +366,7 @@
         spread_traces(new, m, tx_out.at[c], ty_out.at[c])
 
     def move(c):
+        arrived(0, c)
         update(0, c)
         sums = (zero, zero)
         q0j = planes[1]
@@ -374,7 +380,6 @@
         send_faces(1, c)
 
     def back(c):
-        update(1, c)
         q0j = planes[1]
         for i in range(0, N, 2):
             values = []
@@ -382,9 +387,8 @@
                 add = table[1, i + n] * tx_out[c, n] + q0j * ty_out[c, i + n : i + n + 1, :]
                 values.append(u_out[c, i + n] + g_out[c, i + n] * add)
             a, b = pair_y(lyi_c[...], *values)
-            t_scr[pl.ds(i, 32, stride=STRIDE), :] = a
-            t_scr[pl.ds(i + 1, 32, stride=STRIDE), :] = b
-        x_either(t_scr, x_out.at[c], lx_c[...])
+            y_out[c, pl.ds(i, 32, stride=STRIDE), :] = a
+            y_out[c, pl.ds(i + 1, 32, stride=STRIDE), :] = b
 
     for c in range(COMPS):
         forward(c)
@@ -392,7 +396,12 @@
         from_present(d, mcopy(d).wait_recv)
     for c in range(COMPS):
         move(c)
+    arrived(1, 0)
+    update(1, 0)
     for c in range(COMPS):
+        if c + 1 < COMPS:
+            arrived(1, c + 1)
+            update(1, c + 1)
         back(c)
     for d in range(4):
         where_present(d, mcopy(d).wait_send)
@@ -405,7 +414,7 @@
 CHUNKS = 4
 
 
-def back_kernel(x_ref, wz_c, out_hbm, o_scr, out_sem):
+def back_kernel(y_ref, lx_c, wz_c, out_hbm, x_scr, o_scr, out_sem):
     def ocopy(c, chunk, side):
         first = chunk * 512 if side == 0 else 3584 - chunk * 512
         return pltpu.make_async_copy(
@@ -415,9 +424,10 @@
         )
 
     for c in range(COMPS):
+        x_either(y_ref.at[c], x_scr.at[c], lx_c[...])
         for chunk in range(CHUNKS):
             for p in range(4 * chunk, 4 * chunk + 4):
-                z_back(x_ref.at[c], o_scr.at[c], wz_c[...], p)
+                z_back(x_scr.at[c], o_scr.at[c], wz_c[...], p)
             ocopy(c, chunk, 0).start()
             ocopy(c, chunk, 1).start()
     for c in range(COMPS):
@@ -433,7 +443,7 @@
     smem = pl.BlockSpec(memory_space=pltpu.SMEM)
     hbm = pl.BlockSpec(memory_space=pltpu.HBM)
     spectral = (COMPS, N, N // 2, 128)
-    x_back = pl.pallas_call(
+    y_back = pl.pallas_call(
         trace_kernel,
         out_shape=pltpu.VMEM((COMPS, 32 * STRIDE, 128), F32),
         in_specs=[hbm, hbm, smem] + [hbm] * 7,
@@ -477,16 +487,17 @@
     out = pl.pallas_call(
         back_kernel,
         out_shape=jax.ShapeDtypeStruct((COMPS, N, N * N), F32),
-        in_specs=[vmem] * 2,
+        in_specs=[vmem] * 3,
         out_specs=hbm,
         scratch_shapes=[
+            pltpu.VMEM((COMPS, 32 * STRIDE, 128), F32),
             pltpu.VMEM((COMPS, N, N * N), F32),
             pltpu.SemaphoreType.DMA((COMPS, CHUNKS, 2)),
         ],
         compiler_params=pltpu.CompilerParams(vmem_limit_bytes=40 * 2**20),
         cost_estimate=pl.CostEstimate(flops=2 * 10**9, bytes_accessed=3 * 2**20, transcendentals=0),
         name="back",
-    )(x_back, wz)
+    )(y_back, lx, wz)
     return out.reshape(forcing.shape)
 
 

time: 21.1 us -> 21.4 us (1.014)
  Pallas kernels: 20.3 us -> 20.6 us
    pallas_call x1, Pallas kernels: 2.1 us -> 2.9 us  [shards(): pl.pallas_call(back_kernel, out_shape=jax.ShapeDtypeStruct((COMPS, N, N *...]
    pallas_call x1, Pallas kernels: 18.2 us -> 17.7 us  [shards(): pl.pallas_call(trace_kernel, out_shape=pltpu.VMEM((COMPS, 32 * STRIDE, 12...]
where the time goes in v3:
time: 21.4 us; the launch traced here: 21.3 us
  Pallas kernels  20.6 us (96%)
  between operations  0.69 us (3%)
    pallas_call x1, Pallas kernels, shards(): pl.pallas_call(trace_kernel, out_shape=pltpu.VMEM((COMPS, 32 * STRIDE, 12...  17.7 us
    pallas_call x1, Pallas kernels, shards(): pl.pallas_call(back_kernel, out_shape=jax.ShapeDtypeStruct((COMPS, N, N *...  2.9 us

profile of v3, /device:TPU:24, one launch (start us, length us, event | category | flops | bytes accessed | tf_op | source)
XLA Modules:
  0.0 21.3 jit_solution(5248218996203499118)
XLA Ops:
  0.7 0.0 copy-start
  0.7 0.0 copy-start.1
  0.7 17.7 %traces.1.y_ref = f32[3,2304,128]{2,1,0:T(8,128)S(1)} custom-call(f32[3,64,4096]{2,1,0:T(8,128)} %bitcast.2, f32[1,1,3]{2,1,0:T(1,128)} %mod_h.1, s32[1,1]{1,0:T(1,128)S(6)} %copy.11.codes, f32[3,64]{1,0:T(4,128)} %constant.19.clone.table_h, bf16[64,192]{1,0:T(8,128)(2,1)} %constant.14.clone.lx_h.lx_c, bf16[64,96]{1,0:T(8,128)(2,1)} %constant.15.clone.ly_h, ...), custom_call_target="tpu_custom_call" | custom-call | flops 2000000000 | bytes 3145728 | tf_op jit(solution)/shard_map/traces/pallas_call | solution.py:446
  18.4 0.0 copy-done
  18.4 0.0 copy-done.1
  18.4 2.9 %back.1 = f32[3,64,4096]{2,1,0:T(8,128)} custom-call(f32[3,2304,128]{2,1,0:T(8,128)S(1)} %traces.1.y_ref, bf16[64,192]{1,0:T(8,128)(2,1)S(1)} %copy-done.1, bf16[256,256]{1,0:T(8,128)(2,1)S(1)} %copy-done), custom_call_target="tpu_custom_call" | custom-call | flops 2000000000 | bytes 3145728 | tf_op jit(solution)/shard_map/back/pallas_call | solution.py:487
Async XLA Ops:
  0.7 17.7 %copy-start = (bf16[256,256]{1,0:T(8,128)(2,1)S(1)}, bf16[256,256]{1,0:T(8,128)(2,1)}, u32[]{:S(2)}) copy-start(bf16[256,256]{1,0:T(8,128)(2,1)} %constant.17.clone.wz_h.wz_c) | copy-start | bytes 393220
  0.7 17.7 %copy-start.1 = (bf16[64,192]{1,0:T(8,128)(2,1)S(1)}, bf16[64,192]{1,0:T(8,128)(2,1)}, u32[]{:S(2)}) copy-start(bf16[64,192]{1,0:T(8,128)(2,1)} %constant.14.clone.lx_h.lx_c) | copy-start | bytes 73732

commit v4 on v3

--- a/solution.py
+++ b/solution.py
@@ -183,7 +183,7 @@
 
 def trace_kernel(
     f_hbm, mod_h, codes, table_h, lx_h, ly_h, lyi_h, wz_h, mx_h, planes_h,
-    y_out,
+    x_out, o_out,
     mod, table, lx_c, ly_c, lyi_c, wz_c, mx_c, planes, u_out, g_out, tx_out, ty_out,
     xin, t_scr, x_scr, y_scr, face, lam, msend, mrecv, send, recv,
     in_sem, con_sem, msend_sem, mrecv_sem, send_sem, recv_sem,
@@ -285,23 +285,14 @@
         for d in range(4):
             where_present(d, gcopy(k, c, d).start)
 
-    def reduce_group(values, base, carry):
-        se, so = carry
-        cj = planes[0]
-        sums = []
-        for n, u in enumerate(values):
-            weighted = table[0, base + n] * u
-            if n % 2 == 0:
-                se = se + weighted
-            else:
-                so = so + weighted
-            w = cj * u
-            sums.append((w[0:8] + w[8:16]) + (w[16:24] + w[24:32]))
-        y = jnp.sum(jnp.stack(sums, axis=0), axis=1)
-        y_scr[base : base + 8, :] = y
-        return se, so
-
-    zero = jnp.zeros((32, 128), F32)
+    def reduce_one(u, i, sums, rows):
+        weighted = table[0, i] * u
+        sums[i % 2] = weighted if sums[i % 2] is None else sums[i % 2] + weighted
+        w = planes[0] * u
+        rows.append((w[0:8] + w[8:16]) + (w[16:24] + w[24:32]))
+        if len(rows) == 8:
+            y_scr[i - 7 : i + 1, :] = jnp.sum(jnp.stack(rows, axis=0), axis=1)
+            rows.clear()
 
     def forward(c):
         if c == 0:
@@ -318,20 +309,17 @@
             loads[c - 1].wait()
             z_forward(xin.at[c], t_scr, wz_c[...], range(16))
         x_either(t_scr, x_scr, lx_c[...])
-        sums = (zero, zero)
-        for base in range(0, N, 8):
-            values = []
-            for n in range(0, 8, 2):
-                a = x_scr[pl.ds(base + n, 32, stride=STRIDE), :]
-                b = x_scr[pl.ds(base + n + 1, 32, stride=STRIDE), :]
-                for off, h in enumerate(pair_y(ly_c[...], a, b)):
-                    i = base + n + off
-                    if c > 0:
-                        g_out[c, i] = gain(c, i)
-                    u = h * g_out[c, i]
-                    u_out[c, i] = u
-                    values.append(u)
-            sums = reduce_group(values, base, sums)
+        sums, rows = [None, None], []
+        for first in range(0, N, 2):
+            a = x_scr[pl.ds(first, 32, stride=STRIDE), :]
+            b = x_scr[pl.ds(first + 1, 32, stride=STRIDE), :]
+            for i, h in zip((first, first + 1), pair_y(ly_c[...], a, b)):
+                g = g_out[0, i] if c == 0 else gain(c, i)
+                if c > 0:
+                    g_out[c, i] = g
+                u = h * g
+                u_out[c, i] = u
+                reduce_one(u, i, sums, rows)
         face_sums(*sums, y_scr[...], moduli[c], face.at[c], False)
         if c == 0:
             pl.semaphore_wait(barrier, 4 - jnp.where(s > 0, 0, 1) - jnp.where(s < ns - 1, 0, 1))
@@ -368,18 +356,17 @@
     def move(c):
         arrived(0, c)
         update(0, c)
-        sums = (zero, zero)
+        sums, rows = [None, None], []
         q0j = planes[1]
-        for base in range(0, N, 8):
-            values = []
-            for i in range(base, base + 8):
-                add = table[1, i] * tx_out[c, i % 2] + q0j * ty_out[c, i : i + 1, :]
-                values.append(g_out[c, i] * add)
-            sums = reduce_group(values, base, sums)
+        for i in range(N):
+            add = table[1, i] * tx_out[c, i % 2] + q0j * ty_out[c, i : i + 1, :]
+            reduce_one(g_out[c, i] * add, i, sums, rows)
         face_sums(*sums, y_scr[...], moduli[c], face.at[c], True)
         send_faces(1, c)
 
     def back(c):
+        arrived(1, c)
+        update(1, c)
         q0j = planes[1]
         for i in range(0, N, 2):
             values = []
@@ -387,8 +374,12 @@
                 add = table[1, i + n] * tx_out[c, n] + q0j * ty_out[c, i + n : i + n + 1, :]
                 values.append(u_out[c, i + n] + g_out[c, i + n] * add)
             a, b = pair_y(lyi_c[...], *values)
-            y_out[c, pl.ds(i, 32, stride=STRIDE), :] = a
-            y_out[c, pl.ds(i + 1, 32, stride=STRIDE), :] = b
+            t_scr[pl.ds(i, 32, stride=STRIDE), :] = a
+            t_scr[pl.ds(i + 1, 32, stride=STRIDE), :] = b
+        x_either(t_scr, x_scr if c == 0 else x_out.at[c - 1], lx_c[...])
+        if c == 0:
+            for p in range(16):
+                z_back(x_scr, o_out, wz_c[...], p)
 
     for c in range(COMPS):
         forward(c)
@@ -396,12 +387,7 @@
         from_present(d, mcopy(d).wait_recv)
     for c in range(COMPS):
         move(c)
-    arrived(1, 0)
-    update(1, 0)
     for c in range(COMPS):
-        if c + 1 < COMPS:
-            arrived(1, c + 1)
-            update(1, c + 1)
         back(c)
     for d in range(4):
         where_present(d, mcopy(d).wait_send)
@@ -414,26 +400,28 @@
 CHUNKS = 4
 
 
-def back_kernel(y_ref, lx_c, wz_c, out_hbm, x_scr, o_scr, out_sem):
+def back_kernel(x_ref, first_ref, wz_c, out_hbm, o_scr, out_sem, first_sem):
     def ocopy(c, chunk, side):
         first = chunk * 512 if side == 0 else 3584 - chunk * 512
         return pltpu.make_async_copy(
             o_scr.at[c, :, pl.ds(first, 512)],
-            out_hbm.at[c, :, pl.ds(first, 512)],
+            out_hbm.at[c + 1, :, pl.ds(first, 512)],
             out_sem.at[c, chunk, side],
         )
 
-    for c in range(COMPS):
-        x_either(y_ref.at[c], x_scr.at[c], lx_c[...])
+    whole = pltpu.make_async_copy(first_ref, out_hbm.at[0], first_sem)
+    whole.start()
+    for c in range(COMPS - 1):
         for chunk in range(CHUNKS):
             for p in range(4 * chunk, 4 * chunk + 4):
-                z_back(x_scr.at[c], o_scr.at[c], wz_c[...], p)
+                z_back(x_ref.at[c], o_scr.at[c], wz_c[...], p)
             ocopy(c, chunk, 0).start()
             ocopy(c, chunk, 1).start()
-    for c in range(COMPS):
+    for c in range(COMPS - 1):
         for chunk in range(CHUNKS):
             ocopy(c, chunk, 0).wait()
             ocopy(c, chunk, 1).wait()
+    whole.wait()
 
 
 def shards(forcing, modulus, orient_codes):
@@ -443,11 +431,14 @@
     smem = pl.BlockSpec(memory_space=pltpu.SMEM)
     hbm = pl.BlockSpec(memory_space=pltpu.HBM)
     spectral = (COMPS, N, N // 2, 128)
-    y_back = pl.pallas_call(
+    x_back, first = pl.pallas_call(
         trace_kernel,
-        out_shape=pltpu.VMEM((COMPS, 32 * STRIDE, 128), F32),
+        out_shape=[
+            pltpu.VMEM((COMPS - 1, 32 * STRIDE, 128), F32),
+            pltpu.VMEM((N, N * N), F32),
+        ],
         in_specs=[hbm, hbm, smem] + [hbm] * 7,
-        out_specs=vmem,
+        out_specs=[vmem] * 2,
         scratch_shapes=[
             pltpu.SMEM((1, 1, COMPS), F32),
             pltpu.SMEM(table.shape, F32),
@@ -490,14 +481,14 @@
         in_specs=[vmem] * 3,
         out_specs=hbm,
         scratch_shapes=[
-            pltpu.VMEM((COMPS, 32 * STRIDE, 128), F32),
-            pltpu.VMEM((COMPS, N, N * N), F32),
-            pltpu.SemaphoreType.DMA((COMPS, CHUNKS, 2)),
+            pltpu.VMEM((COMPS - 1, N, N * N), F32),
+            pltpu.SemaphoreType.DMA((COMPS - 1, CHUNKS, 2)),
+            pltpu.SemaphoreType.DMA(()),
         ],
         compiler_params=pltpu.CompilerParams(vmem_limit_bytes=40 * 2**20),
         cost_estimate=pl.CostEstimate(flops=2 * 10**9, bytes_accessed=3 * 2**20, transcendentals=0),
         name="back",
-    )(y_back, lx, wz)
+    )(x_back, first, wz)
     return out.reshape(forcing.shape)
 
 

time: 21.4 us -> 20.5 us (0.958)
  Pallas kernels: 20.6 us -> 19.7 us
    pallas_call x1, Pallas kernels: 2.9 us -> 1.8 us  [shards(): pl.pallas_call(back_kernel, out_shape=jax.ShapeDtypeStruct((COMPS, N, N *...]
    pallas_call x1, Pallas kernels: 17.7 us -> 17.9 us  [shards(): pl.pallas_call(trace_kernel, out_shape=[pltpu.VMEM((COMPS - 1, 32 * STRID...]
where the time goes in v4:
time: 20.5 us; the launch traced here: 20.4 us
  Pallas kernels  19.7 us (96%)
  between operations  0.68 us (3%)
    pallas_call x1, Pallas kernels, shards(): pl.pallas_call(trace_kernel, out_shape=[pltpu.VMEM((COMPS - 1, 32 * STRID...  17.9 us
    pallas_call x1, Pallas kernels, shards(): pl.pallas_call(back_kernel, out_shape=jax.ShapeDtypeStruct((COMPS, N, N *...  1.8 us

profile of v4, /device:TPU:24, one launch (start us, length us, event | category | flops | bytes accessed | tf_op | source)
XLA Modules:
  0.0 20.4 jit_solution(16238719467241127126)
XLA Ops:
  0.7 0.0 copy-start
  0.7 17.9 %traces.1 = (f32[2,2304,128]{2,1,0:T(8,128)S(1)}, f32[64,4096]{1,0:T(8,128)S(1)}) custom-call(f32[3,64,4096]{2,1,0:T(8,128)} %bitcast.2, f32[1,1,3]{2,1,0:T(1,128)} %mod_h.1, s32[1,1]{1,0:T(1,128)S(6)} %copy.11.codes, f32[3,64]{1,0:T(4,128)} %constant.19.clone.table_h, bf16[64,192]{1,0:T(8,128)(2,1)} %constant.14.clone.lx_h, ...), custom_call_target="tpu_custom_call" | custom-call | flops 2000000000 | bytes 3145728 | tf_op jit(solution)/shard_map/traces/pallas_call | solution.py:434
  18.6 0.0 copy-done
  18.6 1.8 %back.1 = f32[3,64,4096]{2,1,0:T(8,128)} custom-call(f32[2,2304,128]{2,1,0:T(8,128)S(1)} %get-tuple-element.7.x_ref, f32[64,4096]{1,0:T(8,128)S(1)} %get-tuple-element.8.first_ref, bf16[256,256]{1,0:T(8,128)(2,1)S(1)} %copy-done), custom_call_target="tpu_custom_call" | custom-call | flops 2000000000 | bytes 3145728 | tf_op jit(solution)/shard_map/back/pallas_call | solution.py:478
Async XLA Ops:
  0.7 18.0 %copy-start = (bf16[256,256]{1,0:T(8,128)(2,1)S(1)}, bf16[256,256]{1,0:T(8,128)(2,1)}, u32[]{:S(2)}) copy-start(bf16[256,256]{1,0:T(8,128)(2,1)} %constant.17.clone.wz_h.wz_c) | copy-start | bytes 393220

commit v5 on v4

--- a/solution.py
+++ b/solution.py
@@ -365,8 +365,9 @@
         send_faces(1, c)
 
     def back(c):
-        arrived(1, c)
-        update(1, c)
+        if c != 1:
+            arrived(1, c)
+            update(1, c)
         q0j = planes[1]
         for i in range(0, N, 2):
             values = []
@@ -378,6 +379,8 @@
             t_scr[pl.ds(i + 1, 32, stride=STRIDE), :] = b
         x_either(t_scr, x_scr if c == 0 else x_out.at[c - 1], lx_c[...])
         if c == 0:
+            arrived(1, 1)
+            update(1, 1)
             for p in range(16):
                 z_back(x_scr, o_out, wz_c[...], p)
 

time: 20.5 us -> 20.5 us (level)
  no operation moved by 1% of the time
where the time goes in v5:
time: 20.5 us; the launch traced here: 20.4 us
  Pallas kernels  19.7 us (96%)
  between operations  0.68 us (3%)
    pallas_call x1, Pallas kernels, shards(): pl.pallas_call(trace_kernel, out_shape=[pltpu.VMEM((COMPS - 1, 32 * STRID...  17.9 us
    pallas_call x1, Pallas kernels, shards(): pl.pallas_call(back_kernel, out_shape=jax.ShapeDtypeStruct((COMPS, N, N *...  1.8 us

profile of v5, /device:TPU:24, one launch (start us, length us, event | category | flops | bytes accessed | tf_op | source)
XLA Modules:
  0.0 20.4 jit_solution(8258958395015846019)
XLA Ops:
  0.7 0.0 copy-start
  0.7 17.9 %traces.1 = (f32[2,2304,128]{2,1,0:T(8,128)S(1)}, f32[64,4096]{1,0:T(8,128)S(1)}) custom-call(f32[3,64,4096]{2,1,0:T(8,128)} %bitcast.2, f32[1,1,3]{2,1,0:T(1,128)} %mod_h.1, s32[1,1]{1,0:T(1,128)S(6)} %copy.11.codes, f32[3,64]{1,0:T(4,128)} %constant.19.clone.table_h, bf16[64,192]{1,0:T(8,128)(2,1)} %constant.14.clone.lx_h, ...), custom_call_target="tpu_custom_call" | custom-call | flops 2000000000 | bytes 3145728 | tf_op jit(solution)/shard_map/traces/pallas_call | solution.py:437
  18.6 0.0 copy-done
  18.6 1.8 %back.1 = f32[3,64,4096]{2,1,0:T(8,128)} custom-call(f32[2,2304,128]{2,1,0:T(8,128)S(1)} %get-tuple-element.7.x_ref, f32[64,4096]{1,0:T(8,128)S(1)} %get-tuple-element.8.first_ref, bf16[256,256]{1,0:T(8,128)(2,1)S(1)} %copy-done), custom_call_target="tpu_custom_call" | custom-call | flops 2000000000 | bytes 3145728 | tf_op jit(solution)/shard_map/back/pallas_call | solution.py:481
Async XLA Ops:
  0.7 18.0 %copy-start = (bf16[256,256]{1,0:T(8,128)(2,1)S(1)}, bf16[256,256]{1,0:T(8,128)(2,1)}, u32[]{:S(2)}) copy-start(bf16[256,256]{1,0:T(8,128)(2,1)} %constant.17.clone.wz_h.wz_c) | copy-start | bytes 393220
